TPU v7x, 256 devices: a whole 4x4x8 slice. The times are simulated.
256 devices in a mesh: blk: 16 (over z_lo, y, core), ulysses: 16 (over z_hi, x).
Axes of the slice: x: 4, y: 4, z: 8 (z_hi: 4, z_lo: 2; z = z_hi * 2 + z_lo), core: 2. Of those that a mesh axis runs over, the one named last changes fastest.
Arguments:
- query_tokens: bfloat16 [32768, 4096], P(('blk', 'ulysses')), may hold values from -5 to 5
- key_tokens: bfloat16 [32768, 4096], P(('blk', 'ulysses')), may hold values from -5 to 5
- value_tokens: bfloat16 [32768, 4096], P(('blk', 'ulysses')), may hold values from -5 to 5
- cotangent: bfloat16 [32768, 4096], P(('blk', 'ulysses')), may hold values from -5 to 5
- block_mask: int32 [256, 256], replicated, may hold values from 0 to 1, as said below
Outputs:
- attended: bfloat16 [32768, 4096], P(('blk', 'ulysses'))
- grad_query: bfloat16 [32768, 4096], P(('blk', 'ulysses'))
- grad_key: bfloat16 [32768, 4096], P(('blk', 'ulysses'))
- grad_value: bfloat16 [32768, 4096], P(('blk', 'ulysses'))
Inputs may be any that keep to these rules, and one draw needn't show every extreme that they name: block_mask is symmetric. A span is a run of 16 consecutive blocks. Inside a span, block s attends block s2 exactly when they differ by at most one. A query block attends at most one key block in each other span. The queries of one span attend keys of exactly 7 other spans, and at most 2 distinct key blocks of any other span; in every draw some pairs of spans reach 2.
All inputs are finite; a program needn't handle non-finite values.
Results may differ from a plain program's by a relative error of at most 0.0096.
Values may be sent and summed in bfloat16 or wider, within the bound.
A program may use at most 128 MiB of HBM per device.

v0:
```python
import jax
import jax.numpy as jnp
from jax import lax
from jax.sharding import PartitionSpec as P

HEAD_DIM = 128
BLOCK = 128
NEED = 2


def lists_from(flag_rows, list_width):
    columns = flag_rows.shape[-1]
    ranking = flag_rows * columns + (
        columns - 1 - lax.broadcasted_iota(jnp.int32, flag_rows.shape, flag_rows.ndim - 1)
    )
    values_top, indices = lax.top_k(ranking, list_width)
    return (indices, values_top >= columns)


def segment_add(selector, tensor, form):
    return jnp.einsum(form, selector, tensor, precision=lax.Precision.HIGHEST)


def shards(query_tokens, key_tokens, value_tokens, cotangent, block_mask):
    groups = lax.axis_size("blk")
    group_id = lax.axis_index("blk")
    heads_q, heads_k, heads_v, heads_g = (
        lax.all_to_all(query_tokens, "ulysses", split_axis=1, concat_axis=0, tiled=True),
        lax.all_to_all(key_tokens, "ulysses", split_axis=1, concat_axis=0, tiled=True),
        lax.all_to_all(value_tokens, "ulysses", split_axis=1, concat_axis=0, tiled=True),
        lax.all_to_all(cotangent, "ulysses", split_axis=1, concat_axis=0, tiled=True),
    )
    span_len = heads_q.shape[0] // BLOCK
    local_heads = heads_q.shape[1] // HEAD_DIM
    score_scale = HEAD_DIM ** (-0.5)

    def blocked(tensor):
        return tensor.reshape(span_len, BLOCK, local_heads, HEAD_DIM)

    def tokens_of(tensor):
        return tensor.reshape(span_len * BLOCK, local_heads * HEAD_DIM).astype(jnp.bfloat16)

    q_blocks = blocked(heads_q)
    k_blocks = blocked(heads_k)
    v_blocks = blocked(heads_v)
    g_blocks = blocked(heads_g)
    first_row = group_id * span_len
    my_rows = lax.dynamic_slice_in_dim(block_mask, first_row, span_len, 0)
    my_cols = lax.dynamic_slice_in_dim(block_mask, first_row, span_len, 1)
    own_flags = lax.dynamic_slice_in_dim(my_rows, first_row, span_len, 1)
    own_index, own_valid = lists_from(own_flags, 3)
    others = (lax.broadcasted_iota(jnp.int32, (groups, 1), 0) != group_id).astype(jnp.int32)
    row_cube = my_rows.reshape(span_len, groups, span_len)
    fetch_index, fetch_valid = lists_from(jnp.max(row_cube, axis=0) * others, NEED)
    col_cube = my_cols.reshape(groups, span_len, span_len)
    send_index, send_valid = lists_from(jnp.max(col_cube, axis=1) * others, NEED)
    sent_k = k_blocks[send_index]
    sent_v = v_blocks[send_index]
    fetched_k, fetched_v = (
        lax.all_to_all(sent_k, "blk", split_axis=0, concat_axis=0, tiled=True),
        lax.all_to_all(sent_v, "blk", split_axis=0, concat_axis=0, tiled=True),
    )
    spot_iota = lax.broadcasted_iota(jnp.int32, (groups, NEED, span_len), 2)
    fetch_pick = (fetch_index[:, :, None] == spot_iota).astype(jnp.int32)
    attach = jnp.sum(row_cube.transpose(1, 0, 2)[:, None, :, :] * fetch_pick[:, :, None, :], axis=3)
    attach = attach * fetch_valid[:, :, None].astype(jnp.int32)
    query_pick = jnp.sum(attach * spot_iota, axis=2)
    attach_f = attach.astype(jnp.float32)
    own_k = k_blocks[own_index]
    own_v = v_blocks[own_index]
    own_scores = (
        jnp.einsum("irhd,itchd->ithrc", q_blocks, own_k, preferred_element_type=jnp.float32)
        * score_scale
    )
    own_scores = jnp.where(own_valid[:, :, None, None, None], own_scores, -jnp.inf)
    cross_q = q_blocks[query_pick]
    cross_g = g_blocks[query_pick]
    cross_scores = (
        jnp.einsum("curhd,cukhd->cuhrk", cross_q, fetched_k, preferred_element_type=jnp.float32)
        * score_scale
    )
    cross_scores = jnp.where(fetch_valid[:, :, None, None, None], cross_scores, -jnp.inf)
    tile_peak = jnp.max(cross_scores, axis=4)
    cross_peak = jnp.max(
        jnp.where(attach[:, :, :, None, None] > 0, tile_peak[:, :, None], -jnp.inf), axis=(0, 1)
    )
    row_peak = jnp.maximum(jnp.max(own_scores, axis=(1, 4)), cross_peak)
    own_total = jnp.sum(jnp.exp(own_scores - row_peak[:, None, :, :, None]), axis=(1, 4))
    cross_sums = jnp.sum(jnp.exp(cross_scores - row_peak[query_pick][..., None]), axis=4)
    row_total = own_total + segment_add(attach_f, cross_sums, "cui,cuhr->ihr")
    log_total = row_peak + jnp.log(row_total)
    cross_log = log_total[query_pick]
    own_prob = jnp.exp(own_scores - log_total[:, None, :, :, None])
    cross_prob = jnp.exp(cross_scores - cross_log[..., None])
    own_weights = own_prob.astype(jnp.bfloat16)
    cross_weights = cross_prob.astype(jnp.bfloat16)
    cross_out = jnp.einsum(
        "cuhrk,cukhd->curhd", cross_weights, fetched_v, preferred_element_type=jnp.float32
    )
    output = jnp.einsum("ithrc,itchd->irhd", own_weights, own_v, preferred_element_type=jnp.float32)
    output = output + segment_add(attach_f, cross_out, "cui,curhd->irhd")
    row_delta = jnp.sum(g_blocks.astype(jnp.float32) * output, axis=3).transpose(0, 2, 1)
    cross_delta = row_delta[query_pick]
    own_dprob = jnp.einsum("irhd,itchd->ithrc", g_blocks, own_v, preferred_element_type=jnp.float32)
    own_dscore = (own_prob * (own_dprob - row_delta[:, None, :, :, None])).astype(jnp.bfloat16)
    grad_q = score_scale * jnp.einsum(
        "ithrc,itchd->irhd", own_dscore, own_k, preferred_element_type=jnp.float32
    )
    own_dk = score_scale * jnp.einsum(
        "ithrc,irhd->itchd", own_dscore, q_blocks, preferred_element_type=jnp.float32
    )
    own_dv = jnp.einsum(
        "ithrc,irhd->itchd", own_weights, g_blocks, preferred_element_type=jnp.float32
    )
    empty_grad = jnp.zeros((span_len, BLOCK, local_heads, HEAD_DIM), jnp.float32)
    grad_k = empty_grad.at[own_index].add(own_dk)
    grad_v = empty_grad.at[own_index].add(own_dv)
    cross_dprob = jnp.einsum(
        "curhd,cukhd->cuhrk", cross_g, fetched_v, preferred_element_type=jnp.float32
    )
    cross_dscore = (cross_prob * (cross_dprob - cross_delta[..., None])).astype(jnp.bfloat16)
    cross_dq = score_scale * jnp.einsum(
        "cuhrk,cukhd->curhd", cross_dscore, fetched_k, preferred_element_type=jnp.float32
    )
    grad_q = grad_q + segment_add(attach_f, cross_dq, "cui,curhd->irhd")
    part_k = score_scale * jnp.einsum(
        "cuhrk,curhd->cukhd", cross_dscore, cross_q, preferred_element_type=jnp.float32
    )
    part_v = jnp.einsum(
        "cuhrk,curhd->cukhd", cross_weights, cross_g, preferred_element_type=jnp.float32
    )
    back_k, back_v = (
        lax.all_to_all(part_k, "blk", split_axis=0, concat_axis=0, tiled=True),
        lax.all_to_all(part_v, "blk", split_axis=0, concat_axis=0, tiled=True),
    )
    send_pick = ((send_index[:, :, None] == spot_iota) & send_valid[:, :, None]).astype(jnp.float32)
    grad_k = grad_k + segment_add(send_pick, back_k, "buj,bukhd->jkhd")
    grad_v = grad_v + segment_add(send_pick, back_v, "buj,bukhd->jkhd")
    attended, grad_query, grad_key, grad_value = (
        lax.all_to_all(tokens_of(output), "ulysses", split_axis=0, concat_axis=1, tiled=True),
        lax.all_to_all(tokens_of(grad_q), "ulysses", split_axis=0, concat_axis=1, tiled=True),
        lax.all_to_all(tokens_of(grad_k), "ulysses", split_axis=0, concat_axis=1, tiled=True),
        lax.all_to_all(tokens_of(grad_v), "ulysses", split_axis=0, concat_axis=1, tiled=True),
    )
    return (attended, grad_query, grad_key, grad_value)


def solution(mesh):
    placed = (
        P(("blk", "ulysses"), None),
        P(("blk", "ulysses"), None),
        P(("blk", "ulysses"), None),
        P(("blk", "ulysses"), None),
        P(),
    )
    return jax.shard_map(
        shards,
        mesh=mesh,
        in_specs=placed,
        out_specs=(
            P(("blk", "ulysses"), None),
            P(("blk", "ulysses"), None),
            P(("blk", "ulysses"), None),
            P(("blk", "ulysses"), None),
        ),
        check_vma=False,
    )
```

profile of v0, /device:TPU:56, one launch (start us, length us, event | category | flops | bytes accessed | tf_op | source)
XLA Modules:
  0.0 528.4 jit_solution(7634061339372673453)
XLA Ops:
  3.1 10.1 %all-to-all-start.6 = ((bf16[128,16,256]{0,2,1:T(8,128)(2,1)}), bf16[128,16,256]{0,2,1:T(8,128)(2,1)S(1)}, u32[]{:S(2)}, u32[]{:S(2)}) async-start(bf16[128,16,256]{0,2,1:T(8,128)(2,1)} %bitcast.41), calls=%async_computation.6 | async-start | bytes 2097152 | tf_op jit(solution)/shard_map/all_to_all | solution.py:31
  14.5 27.8 %all-to-all-done.6 = bf16[128,16,256]{0,2,1:T(8,128)(2,1)S(1)} async-done(((bf16[128,16,256]{0,2,1:T(8,128)(2,1)}), bf16[128,16,256]{0,2,1:T(8,128)(2,1)S(1)}, u32[]{:S(2)}, u32[]{:S(2)}) %all-to-all-start.6) | async-done | bytes 1048608 | tf_op jit(solution)/shard_map/all_to_all | solution.py:31
  47.8 20.7 %all-to-all-done = bf16[128,16,256]{0,2,1:T(8,128)(2,1)S(1)} async-done(((bf16[128,16,256]{0,2,1:T(8,128)(2,1)}), bf16[128,16,256]{0,2,1:T(8,128)(2,1)S(1)}, u32[]{:S(2)}, u32[]{:S(2)}) %all-to-all-start) | async-done | bytes 1048608 | tf_op jit(solution)/shard_map/all_to_all | solution.py:30
  68.5 10.5 %all-to-all-start.1 = ((bf16[128,16,256]{0,2,1:T(8,128)(2,1)}), bf16[128,16,256]{0,2,1:T(8,128)(2,1)S(1)}, u32[]{:S(2)}, u32[]{:S(2)}) async-start(bf16[128,16,256]{0,2,1:T(8,128)(2,1)} %bitcast.197), calls=%async_computation.1 | async-start | bytes 2097152 | tf_op jit(solution)/shard_map/all_to_all | solution.py:29
  81.3 18.1 %all-to-all-done.1 = bf16[128,16,256]{0,2,1:T(8,128)(2,1)S(1)} async-done(((bf16[128,16,256]{0,2,1:T(8,128)(2,1)}), bf16[128,16,256]{0,2,1:T(8,128)(2,1)S(1)}, u32[]{:S(2)}, u32[]{:S(2)}) %all-to-all-start.1) | async-done | bytes 1048608 | tf_op jit(solution)/shard_map/all_to_all | solution.py:29
  99.3 10.3 %all-to-all-start.2 = ((bf16[128,16,256]{0,2,1:T(8,128)(2,1)}), bf16[128,16,256]{0,2,1:T(8,128)(2,1)S(1)}, u32[]{:S(2)}, u32[]{:S(2)}) async-start(bf16[128,16,256]{0,2,1:T(8,128)(2,1)} %bitcast.195), calls=%async_computation.2 | async-start | bytes 2097152 | tf_op jit(solution)/shard_map/all_to_all | solution.py:28
  115.1 21.1 %all-to-all-done.2 = bf16[128,16,256]{0,2,1:T(8,128)(2,1)S(1)} async-done(((bf16[128,16,256]{0,2,1:T(8,128)(2,1)}), bf16[128,16,256]{0,2,1:T(8,128)(2,1)S(1)}, u32[]{:S(2)}, u32[]{:S(2)}) %all-to-all-start.2) | async-done | bytes 1048608 | tf_op jit(solution)/shard_map/all_to_all | solution.py:28
  151.1 19.7 %all-to-all-done.3 = bf16[16,2,128,2,128]{4,2,3,1,0:T(8,128)(2,1)} async-done(((bf16[16,2,128,2,128]{4,2,3,1,0:T(8,128)(2,1)}), bf16[16,2,128,2,128]{4,2,3,1,0:T(8,128)(2,1)}, u32[]{:S(2)}, u32[]{:S(2)}) %all-to-all-start.3) | async-done | bytes 2097184 | tf_op jit(solution)/shard_map/all_to_all | solution.py:60
  170.8 5.8 %all-to-all-start.4 = ((bf16[16,2,128,2,128]{2,4,3,1,0:T(8,128)(2,1)}), bf16[16,2,128,2,128]{2,4,3,1,0:T(8,128)(2,1)}, u32[]{:S(2)}, u32[]{:S(2)}) async-start(bf16[16,2,128,2,128]{2,4,3,1,0:T(8,128)(2,1)} %bitcast.190), calls=%async_computation.4 | async-start | bytes 4194304 | tf_op jit(solution)/shard_map/all_to_all | solution.py:61
  217.6 6.2 %convolution_bitcast_fusion.2 = f32[16,2,128,2,128]{2,4,3,1,0:T(8,128)} fusion(bf16[16,2,128,2,128]{2,4,3,1,0:T(8,128)(2,1)} %all-to-all-done.4, f32[16,2,2,128,128]{3,4,2,1,0:T(8,128)} %get-tuple-element.58, f32[16,2,2,128]{3,2,1,0:T(2,128)S(1)} %bitcast.198, pred[16,2]{1,0:T(8,128)(4,1)S(1)} %copy.351), kind=kOutput, calls=%fused_computation.36 | convolution fusion | flops 272629760 | bytes 10518560 | tf_op jit(solution)/shard_map/cuhrk,cukhd->curhd/dot_general | solution.py:97
  237.2 7.9 %multiply_reduce_fusion = (f32[16,128,2]{1,2,0:T(2,128)S(1)}, bf16[16,128,2,128]{1,3,2,0:T(8,128)(2,1)}) fusion(bf16[128,16,256]{0,2,1:T(8,128)(2,1)} %copy-done, f32[16,128,2,128]{1,3,2,0:T(8,128)} %copy.374, bf16[16,3,128,2,128]{4,2,1,3,0:T(8,128)(2,1)} %copy.410, f32[16,2,3,128,128]{4,3,2,1,0:T(8,128)} %get-tuple-element.60, ...), kind=kOutput, calls=%fused_computation.41 | convolution fusion | flops 411561984 | bytes 13664304 | tf_op jit(solution)/shard_map/ithrc,itchd->irhd/dot_general | solution.py:100
  259.2 5.8 %fusion.12 = f32[16,128,2,128]{3,0,2,1:T(8,128)} fusion(f32[16,2,128,2,128]{4,2,3,1,0:T(8,128)S(1)} %multiply_bitcast_fusion.2, s32[16,2,16]{2,1,0:T(2,128)S(1)} %multiply_reduce_fusion.1, s32[16,2]{0,1:T(2,128)S(1)} %get-tuple-element.46), kind=kOutput, calls=%fused_computation.42 | convolution fusion | flops 201327616 | bytes 6293632 | tf_op jit(solution)/shard_map/cui,curhd->irhd/dot_general | solution.py:21
  268.0 6.0 %fusion = bf16[16,3,2,128,128]{3,4,1,2,0:T(8,128)(2,1)S(1)} fusion(f32[16,2,3,128,128]{4,3,2,1,0:T(8,128)} %get-tuple-element.60, f32[16,2,128]{2,1,0:T(2,128)S(1)} %bitcast.203, f32[16,2,128]{2,1,0:T(2,128)S(1)} %copy.365, pred[16,3]{1,0:T(8,128)(4,1)S(1)} %copy.340, bf16[16,3,128,2,128]{4,2,1,3,0:T(8,128)(2,1)} %copy.410, ...), kind=kOutput, calls=%fused_computation.12 | convolution fusion | flops 412090368 | bytes 13664304 | tf_op jit(solution)/shard_map/irhd,itchd->ithrc/dot_general | solution.py:104
  281.2 6.5 %all-to-all-start.7 = ((bf16[16,128,256]{1,2,0:T(8,128)(2,1)}), bf16[16,128,256]{1,2,0:T(8,128)(2,1)S(1)}, u32[]{:S(2)}, u32[]{:S(2)}) async-start(bf16[16,128,256]{1,2,0:T(8,128)(2,1)} %bitcast.193), calls=%async_computation.7 | async-start | bytes 2097152 | tf_op jit(solution)/shard_map/all_to_all | solution.py:141
  287.8 5.8 %multiply_bitcast_fusion.1 = f32[16,2,128,2,128]{4,2,3,1,0:T(8,128)} fusion(bf16[16,2,128,2,128]{2,4,3,1,0:T(8,128)(2,1)} %bitcast.184, bf16[16,2,2,128,128]{3,4,2,1,0:T(8,128)(2,1)} %copy-done.6), kind=kOutput, calls=%fused_computation.26 | convolution fusion | flops 269484032 | bytes 8388608 | tf_op jit(solution)/shard_map/cuhrk,curhd->cukhd/dot_general | solution.py:126
  293.5 24.9 %all-to-all-done.7 = bf16[16,128,256]{1,2,0:T(8,128)(2,1)S(1)} async-done(((bf16[16,128,256]{1,2,0:T(8,128)(2,1)}), bf16[16,128,256]{1,2,0:T(8,128)(2,1)S(1)}, u32[]{:S(2)}, u32[]{:S(2)}) %all-to-all-start.7) | async-done | bytes 1048608 | tf_op jit(solution)/shard_map/all_to_all | solution.py:141
  324.2 5.8 %convolution_bitcast_fusion.1 = f32[16,2,128,2,128]{2,4,3,1,0:T(8,128)} fusion(bf16[16,2,128,2,128]{2,4,3,1,0:T(8,128)(2,1)S(1)} %bitcast.187, f32[16,2,2,128,128]{3,4,2,1,0:T(8,128)} %get-tuple-element.58, f32[16,2,2,128]{3,2,1,0:T(2,128)S(1)} %bitcast.200, pred[16,2]{1,0:T(8,128)(4,1)S(1)} %copy.351), kind=kOutput, calls=%fused_computation.35 | convolution fusion | flops 272629760 | bytes 10518560 | tf_op jit(solution)/shard_map/cuhrk,curhd->cukhd/dot_general | solution.py:129
  329.9 55.9 %all-to-all-done.8 = f32[16,2,128,2,128]{4,2,3,1,0:T(8,128)} async-done(((f32[16,2,128,2,128]{4,2,3,1,0:T(8,128)}), f32[16,2,128,2,128]{4,2,3,1,0:T(8,128)}, u32[]{:S(2)}, u32[]{:S(2)}) %all-to-all-start.8) | async-done | bytes 4194336 | tf_op jit(solution)/shard_map/all_to_all | solution.py:133
  397.3 5.9 %fusion.15 = f32[16,128,2,128]{3,0,2,1:T(8,128)S(1)} fusion(f32[16,2,128,2,128]{4,2,3,1,0:T(8,128)} %all-to-all-done.8, s32[16,2]{0,1:T(2,128)S(1)} %get-tuple-element.52, pred[16,2]{0,1:T(4,128)(4,1)S(1)} %slice_compare_fusion.1), kind=kOutput, calls=%fused_computation.43 | convolution fusion | flops 201327616 | bytes 6291616 | tf_op jit(solution)/shard_map/buj,bukhd->jkhd/dot_general | solution.py:21
  404.4 9.4 %scatter_fusion = f32[16,128,2,128]{3,1,2,0:T(8,128)S(1)} fusion(f32[16,128,2,128]{3,1,2,0:T(8,128)S(1)} %copy.396, s32[48]{0:T(128)S(1)} %reshape.124, f32[48,128,2,128]{3,1,2,0:T(8,128)} %bitcast.183), kind=kCustom, calls=%fused_computation.9 | custom fusion | flops 1572864 | bytes 18874560 | tf_op jit(solution)/shard_map/scatter-add | solution.py:116
  417.2 35.7 %all-to-all-done.10 = f32[16,2,128,2,128]{2,4,3,1,0:T(8,128)} async-done(((f32[16,2,128,2,128]{2,4,3,1,0:T(8,128)}), f32[16,2,128,2,128]{2,4,3,1,0:T(8,128)}, u32[]{:S(2)}, u32[]{:S(2)}) %all-to-all-start.10) | async-done | bytes 4194336 | tf_op jit(solution)/shard_map/all_to_all | solution.py:134
  475.6 9.4 %scatter_fusion.1 = f32[16,128,2,128]{3,1,2,0:T(8,128)S(1)} fusion(f32[16,128,2,128]{3,1,2,0:T(8,128)S(1)} %copy.402, s32[48]{0:T(128)S(1)} %reshape.124, f32[48,128,2,128]{3,1,2,0:T(8,128)} %bitcast.182), kind=kCustom, calls=%fused_computation.10 | custom fusion | flops 1572864 | bytes 18874560 | tf_op jit(solution)/shard_map/scatter-add | solution.py:117
  488.9 7.3 %all-to-all-start.11 = ((bf16[16,128,256]{1,2,0:T(8,128)(2,1)}), bf16[16,128,256]{1,2,0:T(8,128)(2,1)S(1)}, u32[]{:S(2)}, u32[]{:S(2)}) async-start(bf16[16,128,256]{1,2,0:T(8,128)(2,1)} %bitcast.78), calls=%async_computation.11 | async-start | bytes 2097152 | tf_op jit(solution)/shard_map/all_to_all | solution.py:143
  502.0 24.8 %all-to-all-done.11 = bf16[16,128,256]{1,2,0:T(8,128)(2,1)S(1)} async-done(((bf16[16,128,256]{1,2,0:T(8,128)(2,1)}), bf16[16,128,256]{1,2,0:T(8,128)(2,1)S(1)}, u32[]{:S(2)}, u32[]{:S(2)}) %all-to-all-start.11) | async-done | bytes 1048608 | tf_op jit(solution)/shard_map/all_to_all | solution.py:143
  (128 shorter events, 165.7 us)
Async XLA Ops:
  0.6 12.6 %copy-start.11 = (bf16[128,4096]{1,0:T(8,128)(2,1)S(1)}, bf16[128,4096]{1,0:T(8,128)(2,1)}, u32[]{:S(2)}) copy-start(bf16[128,4096]{1,0:T(8,128)(2,1)} %param.7) | copy-start | bytes 3145732
  0.6 45.8 %copy-start.12 = (bf16[128,4096]{1,0:T(8,128)(2,1)S(1)}, bf16[128,4096]{1,0:T(8,128)(2,1)}, u32[]{:S(2)}) copy-start(bf16[128,4096]{1,0:T(8,128)(2,1)} %param.6) | copy-start | bytes 3145732
  3.1 39.3 %all-to-all-start.6 = ((bf16[128,16,256]{0,2,1:T(8,128)(2,1)}), bf16[128,16,256]{0,2,1:T(8,128)(2,1)S(1)}, u32[]{:S(2)}, u32[]{:S(2)}) async-start(bf16[128,16,256]{0,2,1:T(8,128)(2,1)} %bitcast.41), calls=%async_computation.6 | async-start | bytes 2097152 | tf_op jit(solution)/shard_map/all_to_all | solution.py:31
  42.3 38.9 %copy-start = (bf16[128,16,256]{0,2,1:T(8,128)(2,1)}, bf16[128,16,256]{0,2,1:T(8,128)(2,1)S(1)}, u32[]{:S(2)}) copy-start(bf16[128,16,256]{0,2,1:T(8,128)(2,1)S(1)} %all-to-all-done.6) | copy-start | bytes 3145732
  42.3 26.2 %all-to-all-start = ((bf16[128,16,256]{0,2,1:T(8,128)(2,1)}), bf16[128,16,256]{0,2,1:T(8,128)(2,1)S(1)}, u32[]{:S(2)}, u32[]{:S(2)}) async-start(bf16[128,16,256]{0,2,1:T(8,128)(2,1)} %bitcast), calls=%async_computation | async-start | bytes 2097152 | tf_op jit(solution)/shard_map/all_to_all | solution.py:30
  46.4 63.2 %copy-start.13 = (s32[256,256]{1,0:T(8,128)S(1)}, s32[256,256]{1,0:T(8,128)}, u32[]{:S(2)}) copy-start(s32[256,256]{1,0:T(8,128)} %param.9) | copy-start | bytes 786436
  68.5 30.9 %all-to-all-start.1 = ((bf16[128,16,256]{0,2,1:T(8,128)(2,1)}), bf16[128,16,256]{0,2,1:T(8,128)(2,1)S(1)}, u32[]{:S(2)}, u32[]{:S(2)}) async-start(bf16[128,16,256]{0,2,1:T(8,128)(2,1)} %bitcast.197), calls=%async_computation.1 | async-start | bytes 2097152 | tf_op jit(solution)/shard_map/all_to_all | solution.py:29
  99.3 36.9 %all-to-all-start.2 = ((bf16[128,16,256]{0,2,1:T(8,128)(2,1)}), bf16[128,16,256]{0,2,1:T(8,128)(2,1)S(1)}, u32[]{:S(2)}, u32[]{:S(2)}) async-start(bf16[128,16,256]{0,2,1:T(8,128)(2,1)} %bitcast.195), calls=%async_computation.2 | async-start | bytes 2097152 | tf_op jit(solution)/shard_map/all_to_all | solution.py:28
  136.2 10.8 %copy-start.2 = (bf16[128,16,256]{0,2,1:T(8,128)(2,1)}, bf16[128,16,256]{0,2,1:T(8,128)(2,1)S(1)}, u32[]{:S(2)}) copy-start(bf16[128,16,256]{0,2,1:T(8,128)(2,1)S(1)} %all-to-all-done.2) | copy-start | bytes 3145732
  136.2 34.6 %all-to-all-start.3 = ((bf16[16,2,128,2,128]{4,2,3,1,0:T(8,128)(2,1)}), bf16[16,2,128,2,128]{4,2,3,1,0:T(8,128)(2,1)}, u32[]{:S(2)}, u32[]{:S(2)}) async-start(bf16[16,2,128,2,128]{4,2,3,1,0:T(8,128)(2,1)} %bitcast.191), calls=%async_computation.3 | async-start | bytes 4194304 | tf_op jit(solution)/shard_map/all_to_all | solution.py:60
  170.8 46.8 %all-to-all-start.4 = ((bf16[16,2,128,2,128]{2,4,3,1,0:T(8,128)(2,1)}), bf16[16,2,128,2,128]{2,4,3,1,0:T(8,128)(2,1)}, u32[]{:S(2)}, u32[]{:S(2)}) async-start(bf16[16,2,128,2,128]{2,4,3,1,0:T(8,128)(2,1)} %bitcast.190), calls=%async_computation.4 | async-start | bytes 4194304 | tf_op jit(solution)/shard_map/all_to_all | solution.py:61
  198.6 5.0 copy-start.4
  245.2 36.1 %all-to-all-start.5 = ((bf16[16,128,256]{1,2,0:T(8,128)(2,1)}), bf16[16,128,256]{1,2,0:T(8,128)(2,1)}, u32[]{:S(2)}, u32[]{:S(2)}) async-start(bf16[16,128,256]{1,2,0:T(8,128)(2,1)} %bitcast.192), calls=%async_computation.5 | async-start | bytes 2097152 | tf_op jit(solution)/shard_map/all_to_all | solution.py:140
  268.0 7.6 %copy-start.8 = (f32[16,128,2,128]{1,3,2,0:T(8,128)S(1)}, f32[16,128,2,128]{1,3,2,0:T(8,128)}, u32[]{:S(2)}) copy-start(f32[16,128,2,128]{1,3,2,0:T(8,128)} %copy.389) | copy-start | bytes 6291460
  281.2 37.2 %all-to-all-start.7 = ((bf16[16,128,256]{1,2,0:T(8,128)(2,1)}), bf16[16,128,256]{1,2,0:T(8,128)(2,1)S(1)}, u32[]{:S(2)}, u32[]{:S(2)}) async-start(bf16[16,128,256]{1,2,0:T(8,128)(2,1)} %bitcast.193), calls=%async_computation.7 | async-start | bytes 2097152 | tf_op jit(solution)/shard_map/all_to_all | solution.py:141
  293.5 30.6 %copy-start.5 = (bf16[32,128,2,128]{1,3,2,0:T(8,128)(2,1)S(1)}, bf16[32,128,2,128]{1,3,2,0:T(8,128)(2,1)}, u32[]{:S(2)}) copy-start(bf16[32,128,2,128]{1,3,2,0:T(8,128)(2,1)} %gather_fusion.7) | copy-start | bytes 6291460
  318.4 11.5 %copy-start.9 = (bf16[16,128,256]{1,2,0:T(8,128)(2,1)}, bf16[16,128,256]{1,2,0:T(8,128)(2,1)S(1)}, u32[]{:S(2)}) copy-start(bf16[16,128,256]{1,2,0:T(8,128)(2,1)S(1)} %all-to-all-done.7) | copy-start | bytes 3145732
  318.4 67.4 %all-to-all-start.8 = ((f32[16,2,128,2,128]{4,2,3,1,0:T(8,128)}), f32[16,2,128,2,128]{4,2,3,1,0:T(8,128)}, u32[]{:S(2)}, u32[]{:S(2)}) async-start(f32[16,2,128,2,128]{4,2,3,1,0:T(8,128)} %multiply_bitcast_fusion.1), calls=%async_computation.8 | async-start | bytes 8388608 | tf_op jit(solution)/shard_map/all_to_all | solution.py:133
  329.9 61.3 %copy-start.3 = (bf16[128,16,256]{0,2,1:T(8,128)(2,1)S(1)}, bf16[128,16,256]{0,2,1:T(8,128)(2,1)}, u32[]{:S(2)}) copy-start(bf16[128,16,256]{0,2,1:T(8,128)(2,1)} %copy-done.2) | copy-start | bytes 3145732
  385.8 67.1 %all-to-all-start.10 = ((f32[16,2,128,2,128]{2,4,3,1,0:T(8,128)}), f32[16,2,128,2,128]{2,4,3,1,0:T(8,128)}, u32[]{:S(2)}, u32[]{:S(2)}) async-start(f32[16,2,128,2,128]{2,4,3,1,0:T(8,128)} %convolution_bitcast_fusion.1), calls=%async_computation.10 | async-start | bytes 8388608 | tf_op jit(solution)/shard_map/all_to_all | solution.py:134
  413.8 43.7 %copy-start.1 = (bf16[128,16,256]{0,2,1:T(8,128)(2,1)S(1)}, bf16[128,16,256]{0,2,1:T(8,128)(2,1)}, u32[]{:S(2)}) copy-start(bf16[128,16,256]{0,2,1:T(8,128)(2,1)} %copy-done) | copy-start | bytes 3145732
  452.9 36.0 %all-to-all-start.9 = ((bf16[16,128,256]{1,2,0:T(8,128)(2,1)}), bf16[16,128,256]{1,2,0:T(8,128)(2,1)}, u32[]{:S(2)}, u32[]{:S(2)}) async-start(bf16[16,128,256]{1,2,0:T(8,128)(2,1)} %bitcast.68), calls=%async_computation.9 | async-start | bytes 2097152 | tf_op jit(solution)/shard_map/all_to_all | solution.py:142
  485.2 13.3 %copy-start.10 = (bf16[16,128,256]{1,2,0:T(8,128)(2,1)S(1)}, bf16[16,128,256]{1,2,0:T(8,128)(2,1)}, u32[]{:S(2)}) copy-start(bf16[16,128,256]{1,2,0:T(8,128)(2,1)} %copy-done.9) | copy-start | bytes 3145732
  488.9 37.9 %all-to-all-start.11 = ((bf16[16,128,256]{1,2,0:T(8,128)(2,1)}), bf16[16,128,256]{1,2,0:T(8,128)(2,1)S(1)}, u32[]{:S(2)}, u32[]{:S(2)}) async-start(bf16[16,128,256]{1,2,0:T(8,128)(2,1)} %bitcast.78), calls=%async_computation.11 | async-start | bytes 2097152 | tf_op jit(solution)/shard_map/all_to_all | solution.py:143
  (2 other events, 4.9 us)
where the time goes:
time: 534 us; the launch traced here: 528 us
  waiting for transfers between devices  254 us (48%)
  local copies, waits for them, and re-layouts  82.5 us (15%)
  starting transfers between devices  80.7 us (15%)
  matrix products  79.8 us (15%)
  other arithmetic  29.6 us (6%)
    all_to_all x1, waiting for transfers between devices, shards(): lax.all_to_all(part_k, 'blk', split_axis=0, concat_axis=0, tiled=True)  55.9 us
    all_to_all x1, waiting for transfers between devices, shards(): lax.all_to_all(part_v, 'blk', split_axis=0, concat_axis=0, tiled=True)  35.7 us
    all_to_all x1, waiting for transfers between devices, shards(): lax.all_to_all(cotangent, 'ulysses', split_axis=1, concat_axis=0, tiled=T...  27.8 us
    all_to_all x1, waiting for transfers between devices, shards(): lax.all_to_all(tokens_of(grad_q), 'ulysses', split_axis=0, concat_axis=1,...  24.9 us
    all_to_all x1, waiting for transfers between devices, shards(): lax.all_to_all(tokens_of(grad_v), 'ulysses', split_axis=0, concat_axis=1,...  24.8 us
    all_to_all x1, waiting for transfers between devices, shards(): lax.all_to_all(query_tokens, 'ulysses', split_axis=1, concat_axis=0, tile...  21.1 us
    dot_general x5, matrix products, segment_add(): return jnp.einsum(form, selector, tensor, precision=lax.Precision.HIGHEST)  20.8 us
    all_to_all x1, waiting for transfers between devices, shards(): lax.all_to_all(value_tokens, 'ulysses', split_axis=1, concat_axis=0, tile...  20.7 us
  transfers between devices with their start and end apart: 12, of which 11 were waited for; matrix products, arithmetic and copies ran while one was open for 30% of the time, Pallas kernels for 0%

commit v1 on v0

--- a/solution.py
+++ b/solution.py
@@ -28,7 +28,12 @@
         lax.all_to_all(query_tokens, "ulysses", split_axis=1, concat_axis=0, tiled=True),
         lax.all_to_all(key_tokens, "ulysses", split_axis=1, concat_axis=0, tiled=True),
         lax.all_to_all(value_tokens, "ulysses", split_axis=1, concat_axis=0, tiled=True),
-        lax.all_to_all(cotangent, "ulysses", split_axis=1, concat_axis=0, tiled=True),
+        jnp.concatenate(
+            lax.all_to_all(
+                jnp.stack(jnp.split(cotangent, lax.axis_size("ulysses"), axis=1)), "ulysses", 0, 0
+            ),
+            axis=0,
+        ),
     )
     span_len = heads_q.shape[0] // BLOCK
     local_heads = heads_q.shape[1] // HEAD_DIM

time: 534 us -> 565 us (1.058)
  local copies, waits for them, and re-layouts: 82.5 us -> 109 us
    unnamed x33 -> x48, local copies, waits for them, and re-layouts: 10.1 us -> 32.3 us
  transfers between devices with their start and end apart: 12 -> 12, of which waited for: 11 -> 10; matrix products, arithmetic and copies ran while one was open for 30% -> 30% of each run, Pallas kernels for 0% -> 0%
where the time goes in v1:
time: 565 us; the launch traced here: 558 us
  waiting for transfers between devices  252 us (45%)
  local copies, waits for them, and re-layouts  109 us (19%)
  starting transfers between devices  83 us (15%)
  matrix products  82.6 us (15%)
  other arithmetic  29.6 us (5%)
    all_to_all x1, waiting for transfers between devices, shards(): lax.all_to_all(part_k, 'blk', split_axis=0, concat_axis=0, tiled=True)  55.9 us
    all_to_all x1, waiting for transfers between devices, shards(): lax.all_to_all(part_v, 'blk', split_axis=0, concat_axis=0, tiled=True)  35.7 us
    unnamed x48, local copies, waits for them, and re-layouts  32.3 us
    all_to_all x1, waiting for transfers between devices, shards(): lax.all_to_all(jnp.stack(jnp.split(cotangent, lax.axis_size('ulysses'), a...  27.8 us
    all_to_all x1, waiting for transfers between devices, shards(): lax.all_to_all(tokens_of(grad_q), 'ulysses', split_axis=0, concat_axis=1,...  24.9 us
    all_to_all x1, waiting for transfers between devices, shards(): lax.all_to_all(tokens_of(grad_v), 'ulysses', split_axis=0, concat_axis=1,...  24.8 us
    dot_general x5, matrix products, segment_add(): return jnp.einsum(form, selector, tensor, precision=lax.Precision.HIGHEST)  20.8 us
    all_to_all x1, waiting for transfers between devices, shards(): lax.all_to_all(query_tokens, 'ulysses', split_axis=1, concat_axis=0, tile...  20.7 us
  transfers between devices with their start and end apart: 12, of which 10 were waited for; matrix products, arithmetic and copies ran while one was open for 30% of the time, Pallas kernels for 0%

profile of v1, /device:TPU:56, one launch (start us, length us, event | category | flops | bytes accessed | tf_op | source)
XLA Modules:
  0.0 558.0 jit_solution(9600516541435589476)
XLA Ops:
  24.4 10.1 %all-to-all-start.6 = ((bf16[16,128,256]{2,1,0:T(8,128)(2,1)}), bf16[16,128,256]{2,1,0:T(8,128)(2,1)S(1)}, u32[]{:S(2)}, u32[]{:S(2)}) async-start(bf16[16,128,256]{2,1,0:T(8,128)(2,1)} %bitcast_dynamic-update-slice_fusion), calls=%async_computation.6 | async-start | bytes 2097152 | tf_op jit(solution)/shard_map/all_to_all | solution.py:32
  35.8 27.8 %all-to-all-done.6 = bf16[16,128,256]{2,1,0:T(8,128)(2,1)S(1)} async-done(((bf16[16,128,256]{2,1,0:T(8,128)(2,1)}), bf16[16,128,256]{2,1,0:T(8,128)(2,1)S(1)}, u32[]{:S(2)}, u32[]{:S(2)}) %all-to-all-start.6) | async-done | bytes 1048608 | tf_op jit(solution)/shard_map/all_to_all | solution.py:32
  69.1 20.7 %all-to-all-done = bf16[128,16,256]{0,2,1:T(8,128)(2,1)S(1)} async-done(((bf16[128,16,256]{0,2,1:T(8,128)(2,1)}), bf16[128,16,256]{0,2,1:T(8,128)(2,1)S(1)}, u32[]{:S(2)}, u32[]{:S(2)}) %all-to-all-start) | async-done | bytes 1048608 | tf_op jit(solution)/shard_map/all_to_all | solution.py:30
  89.8 10.5 %all-to-all-start.1 = ((bf16[128,16,256]{0,2,1:T(8,128)(2,1)}), bf16[128,16,256]{0,2,1:T(8,128)(2,1)S(1)}, u32[]{:S(2)}, u32[]{:S(2)}) async-start(bf16[128,16,256]{0,2,1:T(8,128)(2,1)} %bitcast.228), calls=%async_computation.1 | async-start | bytes 2097152 | tf_op jit(solution)/shard_map/all_to_all | solution.py:29
  102.6 18.1 %all-to-all-done.1 = bf16[128,16,256]{0,2,1:T(8,128)(2,1)S(1)} async-done(((bf16[128,16,256]{0,2,1:T(8,128)(2,1)}), bf16[128,16,256]{0,2,1:T(8,128)(2,1)S(1)}, u32[]{:S(2)}, u32[]{:S(2)}) %all-to-all-start.1) | async-done | bytes 1048608 | tf_op jit(solution)/shard_map/all_to_all | solution.py:29
  120.6 10.3 %all-to-all-start.2 = ((bf16[128,16,256]{0,2,1:T(8,128)(2,1)}), bf16[128,16,256]{0,2,1:T(8,128)(2,1)S(1)}, u32[]{:S(2)}, u32[]{:S(2)}) async-start(bf16[128,16,256]{0,2,1:T(8,128)(2,1)} %bitcast.226), calls=%async_computation.2 | async-start | bytes 2097152 | tf_op jit(solution)/shard_map/all_to_all | solution.py:28
  136.8 20.7 %all-to-all-done.2 = bf16[128,16,256]{0,2,1:T(8,128)(2,1)S(1)} async-done(((bf16[128,16,256]{0,2,1:T(8,128)(2,1)}), bf16[128,16,256]{0,2,1:T(8,128)(2,1)S(1)}, u32[]{:S(2)}, u32[]{:S(2)}) %all-to-all-start.2) | async-done | bytes 1048608 | tf_op jit(solution)/shard_map/all_to_all | solution.py:28
  171.9 20.2 %all-to-all-done.3 = bf16[16,2,128,2,128]{4,2,3,1,0:T(8,128)(2,1)} async-done(((bf16[16,2,128,2,128]{4,2,3,1,0:T(8,128)(2,1)}), bf16[16,2,128,2,128]{4,2,3,1,0:T(8,128)(2,1)}, u32[]{:S(2)}, u32[]{:S(2)}) %all-to-all-start.3) | async-done | bytes 2097184 | tf_op jit(solution)/shard_map/all_to_all | solution.py:65
  241.4 6.2 %convolution_bitcast_fusion.2 = f32[16,2,128,2,128]{2,4,3,1,0:T(8,128)} fusion(bf16[16,2,128,2,128]{2,4,3,1,0:T(8,128)(2,1)} %all-to-all-done.4, f32[16,2,2,128,128]{3,4,2,1,0:T(8,128)} %get-tuple-element.58, f32[16,2,2,128]{3,2,1,0:T(2,128)S(1)} %bitcast.229, pred[16,2]{1,0:T(8,128)(4,1)S(1)} %copy.351), kind=kOutput, calls=%fused_computation.36 | convolution fusion | flops 272629760 | bytes 10518560 | tf_op jit(solution)/shard_map/cuhrk,cukhd->curhd/dot_general | solution.py:102
  261.0 7.9 %multiply_reduce_fusion = (f32[16,128,2]{1,2,0:T(2,128)S(1)}, bf16[16,128,2,128]{1,3,2,0:T(8,128)(2,1)}) fusion(bf16[16,128,256]{1,2,0:T(8,128)(2,1)} %copy.376, f32[16,128,2,128]{1,3,2,0:T(8,128)} %copy.374, bf16[16,3,128,2,128]{4,2,1,3,0:T(8,128)(2,1)} %copy.410, f32[16,2,3,128,128]{4,3,2,1,0:T(8,128)} %get-tuple-element.60, ...), kind=kOutput, calls=%fused_computation.41 | convolution fusion | flops 411561984 | bytes 13664304 | tf_op jit(solution)/shard_map/ithrc,itchd->irhd/dot_general | solution.py:105
  282.9 5.8 %fusion.12 = f32[16,128,2,128]{3,0,2,1:T(8,128)} fusion(f32[16,2,128,2,128]{4,2,3,1,0:T(8,128)S(1)} %multiply_bitcast_fusion.2, s32[16,2,16]{2,1,0:T(2,128)S(1)} %multiply_reduce_fusion.1, s32[16,2]{0,1:T(2,128)S(1)} %get-tuple-element.46), kind=kOutput, calls=%fused_computation.42 | convolution fusion | flops 201327616 | bytes 6293632 | tf_op jit(solution)/shard_map/cui,curhd->irhd/dot_general | solution.py:21
  291.7 6.0 %fusion = bf16[16,3,2,128,128]{3,4,1,2,0:T(8,128)(2,1)S(1)} fusion(f32[16,2,3,128,128]{4,3,2,1,0:T(8,128)} %get-tuple-element.60, f32[16,2,128]{2,1,0:T(2,128)S(1)} %bitcast.234, f32[16,2,128]{2,1,0:T(2,128)S(1)} %copy.365, pred[16,3]{1,0:T(8,128)(4,1)S(1)} %copy.340, bf16[16,3,128,2,128]{4,2,1,3,0:T(8,128)(2,1)} %copy.410, ...), kind=kOutput, calls=%fused_computation.12 | convolution fusion | flops 412090368 | bytes 13664304 | tf_op jit(solution)/shard_map/irhd,itchd->ithrc/dot_general | solution.py:109
  304.9 6.5 %all-to-all-start.7 = ((bf16[16,128,256]{1,2,0:T(8,128)(2,1)}), bf16[16,128,256]{1,2,0:T(8,128)(2,1)S(1)}, u32[]{:S(2)}, u32[]{:S(2)}) async-start(bf16[16,128,256]{1,2,0:T(8,128)(2,1)} %bitcast.224), calls=%async_computation.7 | async-start | bytes 2097152 | tf_op jit(solution)/shard_map/all_to_all | solution.py:146
  317.2 24.9 %all-to-all-done.7 = bf16[16,128,256]{1,2,0:T(8,128)(2,1)S(1)} async-done(((bf16[16,128,256]{1,2,0:T(8,128)(2,1)}), bf16[16,128,256]{1,2,0:T(8,128)(2,1)S(1)}, u32[]{:S(2)}, u32[]{:S(2)}) %all-to-all-start.7) | async-done | bytes 1048608 | tf_op jit(solution)/shard_map/all_to_all | solution.py:146
  347.9 5.8 %convolution_bitcast_fusion.1 = f32[16,2,128,2,128]{2,4,3,1,0:T(8,128)} fusion(bf16[16,2,128,2,128]{2,4,3,1,0:T(8,128)(2,1)S(1)} %bitcast.218, f32[16,2,2,128,128]{3,4,2,1,0:T(8,128)} %get-tuple-element.58, f32[16,2,2,128]{3,2,1,0:T(2,128)S(1)} %bitcast.231, pred[16,2]{1,0:T(8,128)(4,1)S(1)} %copy.351), kind=kOutput, calls=%fused_computation.35 | convolution fusion | flops 272629760 | bytes 10518560 | tf_op jit(solution)/shard_map/cuhrk,curhd->cukhd/dot_general | solution.py:134
  353.6 55.9 %all-to-all-done.8 = f32[16,2,128,2,128]{4,2,3,1,0:T(8,128)} async-done(((f32[16,2,128,2,128]{4,2,3,1,0:T(8,128)}), f32[16,2,128,2,128]{4,2,3,1,0:T(8,128)}, u32[]{:S(2)}, u32[]{:S(2)}) %all-to-all-start.8) | async-done | bytes 4194336 | tf_op jit(solution)/shard_map/all_to_all | solution.py:138
  421.0 5.9 %fusion.15 = f32[16,128,2,128]{3,0,2,1:T(8,128)S(1)} fusion(f32[16,2,128,2,128]{4,2,3,1,0:T(8,128)} %all-to-all-done.8, s32[16,2]{0,1:T(2,128)S(1)} %get-tuple-element.52, pred[16,2]{0,1:T(4,128)(4,1)S(1)} %slice_compare_fusion.1), kind=kOutput, calls=%fused_computation.43 | convolution fusion | flops 201327616 | bytes 6291616 | tf_op jit(solution)/shard_map/buj,bukhd->jkhd/dot_general | solution.py:21
  428.1 9.4 %scatter_fusion = f32[16,128,2,128]{3,1,2,0:T(8,128)S(1)} fusion(f32[16,128,2,128]{3,1,2,0:T(8,128)S(1)} %copy.396, s32[48]{0:T(128)S(1)} %reshape.116, f32[48,128,2,128]{3,1,2,0:T(8,128)} %bitcast.214), kind=kCustom, calls=%fused_computation.9 | custom fusion | flops 1572864 | bytes 18874560 | tf_op jit(solution)/shard_map/scatter-add | solution.py:121
  440.9 35.7 %all-to-all-done.10 = f32[16,2,128,2,128]{2,4,3,1,0:T(8,128)} async-done(((f32[16,2,128,2,128]{2,4,3,1,0:T(8,128)}), f32[16,2,128,2,128]{2,4,3,1,0:T(8,128)}, u32[]{:S(2)}, u32[]{:S(2)}) %all-to-all-start.10) | async-done | bytes 4194336 | tf_op jit(solution)/shard_map/all_to_all | solution.py:139
  481.2 6.9 %convolution_bitcast_fusion = f32[16,3,128,2,128]{2,4,1,3,0:T(8,128)} fusion(bf16[16,128,2,128,1]{1,3,4,2,0:T(8,128)(2,1)S(1)} %bitcast.213, f32[16,2,3,128,128]{4,3,2,1,0:T(8,128)} %get-tuple-element.60, f32[16,2,128]{2,1,0:T(2,128)S(1)} %copy.365, pred[16,3]{1,0:T(8,128)(4,1)S(1)} %copy.340), kind=kOutput, calls=%fused_computation.34 | convolution fusion | flops 408944640 | bytes 13647920 | tf_op jit(solution)/shard_map/ithrc,irhd->itchd/dot_general | solution.py:117
  488.1 6.6 %copy.401 = f32[16,3,128,2,128]{4,2,3,1,0:T(8,128)} copy(f32[16,3,128,2,128]{2,4,1,3,0:T(8,128)} %convolution_bitcast_fusion) | data formatting | bytes 12582912 | tf_op jit(solution)/shard_map/ithrc,irhd->itchd/transpose | solution.py:117
  505.3 9.4 %scatter_fusion.1 = f32[16,128,2,128]{3,1,2,0:T(8,128)S(1)} fusion(f32[16,128,2,128]{3,1,2,0:T(8,128)S(1)} %copy.402, s32[48]{0:T(128)S(1)} %reshape.116, f32[48,128,2,128]{3,1,2,0:T(8,128)} %bitcast.203), kind=kCustom, calls=%fused_computation.10 | custom fusion | flops 1572864 | bytes 18874560 | tf_op jit(solution)/shard_map/scatter-add | solution.py:122
  516.2 9.7 %all-to-all-start.11 = ((bf16[16,128,256]{1,2,0:T(8,128)(2,1)}), bf16[16,128,256]{1,2,0:T(8,128)(2,1)S(1)}, u32[]{:S(2)}, u32[]{:S(2)}) async-start(bf16[16,128,256]{1,2,0:T(8,128)(2,1)} %bitcast.92), calls=%async_computation.11 | async-start | bytes 2097152 | tf_op jit(solution)/shard_map/all_to_all | solution.py:148
  531.7 24.8 %all-to-all-done.11 = bf16[16,128,256]{1,2,0:T(8,128)(2,1)S(1)} async-done(((bf16[16,128,256]{1,2,0:T(8,128)(2,1)}), bf16[16,128,256]{1,2,0:T(8,128)(2,1)S(1)}, u32[]{:S(2)}, u32[]{:S(2)}) %all-to-all-start.11) | async-done | bytes 1048608 | tf_op jit(solution)/shard_map/all_to_all | solution.py:148
  (143 shorter events, 190.8 us)
Async XLA Ops:
  0.6 33.9 %copy-start.11 = (bf16[128,4096]{1,0:T(8,128)(2,1)S(1)}, bf16[128,4096]{1,0:T(8,128)(2,1)}, u32[]{:S(2)}) copy-start(bf16[128,4096]{1,0:T(8,128)(2,1)} %param.7) | copy-start | bytes 3145732
  0.6 67.1 %copy-start.12 = (bf16[128,4096]{1,0:T(8,128)(2,1)S(1)}, bf16[128,4096]{1,0:T(8,128)(2,1)}, u32[]{:S(2)}) copy-start(bf16[128,4096]{1,0:T(8,128)(2,1)} %param.6) | copy-start | bytes 3145732
  24.4 39.3 %all-to-all-start.6 = ((bf16[16,128,256]{2,1,0:T(8,128)(2,1)}), bf16[16,128,256]{2,1,0:T(8,128)(2,1)S(1)}, u32[]{:S(2)}, u32[]{:S(2)}) async-start(bf16[16,128,256]{2,1,0:T(8,128)(2,1)} %bitcast_dynamic-update-slice_fusion), calls=%async_computation.6 | async-start | bytes 2097152 | tf_op jit(solution)/shard_map/all_to_all | solution.py:32
  63.6 38.9 %copy-start.8 = (bf16[16,128,256]{2,1,0:T(8,128)(2,1)}, bf16[16,128,256]{2,1,0:T(8,128)(2,1)S(1)}, u32[]{:S(2)}) copy-start(bf16[16,128,256]{2,1,0:T(8,128)(2,1)S(1)} %all-to-all-done.6) | copy-start | bytes 3145732
  63.6 26.2 %all-to-all-start = ((bf16[128,16,256]{0,2,1:T(8,128)(2,1)}), bf16[128,16,256]{0,2,1:T(8,128)(2,1)S(1)}, u32[]{:S(2)}, u32[]{:S(2)}) async-start(bf16[128,16,256]{0,2,1:T(8,128)(2,1)} %bitcast), calls=%async_computation | async-start | bytes 2097152 | tf_op jit(solution)/shard_map/all_to_all | solution.py:30
  67.8 63.2 %copy-start.13 = (s32[256,256]{1,0:T(8,128)S(1)}, s32[256,256]{1,0:T(8,128)}, u32[]{:S(2)}) copy-start(s32[256,256]{1,0:T(8,128)} %param.9) | copy-start | bytes 786436
  89.8 30.9 %all-to-all-start.1 = ((bf16[128,16,256]{0,2,1:T(8,128)(2,1)}), bf16[128,16,256]{0,2,1:T(8,128)(2,1)S(1)}, u32[]{:S(2)}, u32[]{:S(2)}) async-start(bf16[128,16,256]{0,2,1:T(8,128)(2,1)} %bitcast.228), calls=%async_computation.1 | async-start | bytes 2097152 | tf_op jit(solution)/shard_map/all_to_all | solution.py:29
  120.6 36.9 %all-to-all-start.2 = ((bf16[128,16,256]{0,2,1:T(8,128)(2,1)}), bf16[128,16,256]{0,2,1:T(8,128)(2,1)S(1)}, u32[]{:S(2)}, u32[]{:S(2)}) async-start(bf16[128,16,256]{0,2,1:T(8,128)(2,1)} %bitcast.226), calls=%async_computation.2 | async-start | bytes 2097152 | tf_op jit(solution)/shard_map/all_to_all | solution.py:28
  157.5 10.3 %copy-start = (bf16[128,16,256]{0,2,1:T(8,128)(2,1)}, bf16[128,16,256]{0,2,1:T(8,128)(2,1)S(1)}, u32[]{:S(2)}) copy-start(bf16[128,16,256]{0,2,1:T(8,128)(2,1)S(1)} %all-to-all-done.2) | copy-start | bytes 3145732
  157.5 34.6 %all-to-all-start.3 = ((bf16[16,2,128,2,128]{4,2,3,1,0:T(8,128)(2,1)}), bf16[16,2,128,2,128]{4,2,3,1,0:T(8,128)(2,1)}, u32[]{:S(2)}, u32[]{:S(2)}) async-start(bf16[16,2,128,2,128]{4,2,3,1,0:T(8,128)(2,1)} %bitcast.222), calls=%async_computation.3 | async-start | bytes 4194304 | tf_op jit(solution)/shard_map/all_to_all | solution.py:65
  192.1 49.3 %all-to-all-start.4 = ((bf16[16,2,128,2,128]{2,4,3,1,0:T(8,128)(2,1)}), bf16[16,2,128,2,128]{2,4,3,1,0:T(8,128)(2,1)}, u32[]{:S(2)}, u32[]{:S(2)}) async-start(bf16[16,2,128,2,128]{2,4,3,1,0:T(8,128)(2,1)} %bitcast.221), calls=%async_computation.4 | async-start | bytes 4194304 | tf_op jit(solution)/shard_map/all_to_all | solution.py:66
  222.3 5.0 copy-start.3
  268.9 36.1 %all-to-all-start.5 = ((bf16[16,128,256]{1,2,0:T(8,128)(2,1)}), bf16[16,128,256]{1,2,0:T(8,128)(2,1)}, u32[]{:S(2)}, u32[]{:S(2)}) async-start(bf16[16,128,256]{1,2,0:T(8,128)(2,1)} %bitcast.223), calls=%async_computation.5 | async-start | bytes 2097152 | tf_op jit(solution)/shard_map/all_to_all | solution.py:145
  291.7 7.6 %copy-start.7 = (f32[16,128,2,128]{1,3,2,0:T(8,128)S(1)}, f32[16,128,2,128]{1,3,2,0:T(8,128)}, u32[]{:S(2)}) copy-start(f32[16,128,2,128]{1,3,2,0:T(8,128)} %copy.389) | copy-start | bytes 6291460
  304.9 37.2 %all-to-all-start.7 = ((bf16[16,128,256]{1,2,0:T(8,128)(2,1)}), bf16[16,128,256]{1,2,0:T(8,128)(2,1)S(1)}, u32[]{:S(2)}, u32[]{:S(2)}) async-start(bf16[16,128,256]{1,2,0:T(8,128)(2,1)} %bitcast.224), calls=%async_computation.7 | async-start | bytes 2097152 | tf_op jit(solution)/shard_map/all_to_all | solution.py:146
  317.2 30.6 %copy-start.4 = (bf16[32,128,2,128]{1,3,2,0:T(8,128)(2,1)S(1)}, bf16[32,128,2,128]{1,3,2,0:T(8,128)(2,1)}, u32[]{:S(2)}) copy-start(bf16[32,128,2,128]{1,3,2,0:T(8,128)(2,1)} %gather_fusion.7) | copy-start | bytes 6291460
  342.1 11.5 %copy-start.9 = (bf16[16,128,256]{1,2,0:T(8,128)(2,1)}, bf16[16,128,256]{1,2,0:T(8,128)(2,1)S(1)}, u32[]{:S(2)}) copy-start(bf16[16,128,256]{1,2,0:T(8,128)(2,1)S(1)} %all-to-all-done.7) | copy-start | bytes 3145732
  342.1 67.4 %all-to-all-start.8 = ((f32[16,2,128,2,128]{4,2,3,1,0:T(8,128)}), f32[16,2,128,2,128]{4,2,3,1,0:T(8,128)}, u32[]{:S(2)}, u32[]{:S(2)}) async-start(f32[16,2,128,2,128]{4,2,3,1,0:T(8,128)} %multiply_bitcast_fusion.1), calls=%async_computation.8 | async-start | bytes 8388608 | tf_op jit(solution)/shard_map/all_to_all | solution.py:138
  353.6 61.3 %copy-start.1 = (bf16[128,16,256]{0,2,1:T(8,128)(2,1)S(1)}, bf16[128,16,256]{0,2,1:T(8,128)(2,1)}, u32[]{:S(2)}) copy-start(bf16[128,16,256]{0,2,1:T(8,128)(2,1)} %copy-done) | copy-start | bytes 3145732
  409.5 67.1 %all-to-all-start.10 = ((f32[16,2,128,2,128]{2,4,3,1,0:T(8,128)}), f32[16,2,128,2,128]{2,4,3,1,0:T(8,128)}, u32[]{:S(2)}, u32[]{:S(2)}) async-start(f32[16,2,128,2,128]{2,4,3,1,0:T(8,128)} %convolution_bitcast_fusion.1), calls=%async_computation.10 | async-start | bytes 8388608 | tf_op jit(solution)/shard_map/all_to_all | solution.py:139
  437.5 43.7 %copy-start.2 = (bf16[16,128,256]{1,2,0:T(8,128)(2,1)S(1)}, bf16[16,128,256]{1,2,0:T(8,128)(2,1)}, u32[]{:S(2)}) copy-start(bf16[16,128,256]{1,2,0:T(8,128)(2,1)} %copy.376) | copy-start | bytes 3145732
  476.6 39.6 %all-to-all-start.9 = ((bf16[16,128,256]{1,2,0:T(8,128)(2,1)}), bf16[16,128,256]{1,2,0:T(8,128)(2,1)}, u32[]{:S(2)}, u32[]{:S(2)}) async-start(bf16[16,128,256]{1,2,0:T(8,128)(2,1)} %bitcast.81), calls=%async_computation.9 | async-start | bytes 2097152 | tf_op jit(solution)/shard_map/all_to_all | solution.py:147
  514.8 13.3 %copy-start.10 = (bf16[16,128,256]{1,2,0:T(8,128)(2,1)S(1)}, bf16[16,128,256]{1,2,0:T(8,128)(2,1)}, u32[]{:S(2)}) copy-start(bf16[16,128,256]{1,2,0:T(8,128)(2,1)} %copy-done.9) | copy-start | bytes 3145732
  516.2 40.3 %all-to-all-start.11 = ((bf16[16,128,256]{1,2,0:T(8,128)(2,1)}), bf16[16,128,256]{1,2,0:T(8,128)(2,1)S(1)}, u32[]{:S(2)}, u32[]{:S(2)}) async-start(bf16[16,128,256]{1,2,0:T(8,128)(2,1)} %bitcast.92), calls=%async_computation.11 | async-start | bytes 2097152 | tf_op jit(solution)/shard_map/all_to_all | solution.py:148
  (2 other events, 4.9 us)
